TPU v7x, 256 devices: a whole 4x4x8 slice. The times are simulated.
256 devices in a mesh: shot: 8 (over y, core), band: 32 (over x, z).
Axes of the slice: x: 4, y: 4, z: 8, core: 2. Of those that a mesh axis runs over, the one named last changes fastest.
Arguments:
- sensitivity: bfloat16 [16384, 128, 128], P(('shot', 'band')), may hold values from -0.0625 to 0.0625
- bundle_of: int32 [16384], P(('shot', 'band')), may hold values from 0 to 31
- cellblock_of: int32 [16384], P(('shot', 'band')), may hold values from 0 to 15
- state: float32 [65536, 128], P('band'), may hold values from -6 to 6
- prior_velocity: float32 [65536, 128], P('band'), may hold values from -6 to 6
- observed: float32 [256, 128], P(('shot', 'band')), may hold values from -6 to 6
- pick_weight: float32 [256, 128], P(('shot', 'band')), may hold values from 0.3 to 3
Outputs:
- new_state: float32 [65536, 128], P('band')
- weighted_residual: float32 [256, 128, 128], P(('shot', 'band'))
Inputs may be any that keep to these rules, and one draw needn't show every extreme that they name: bundle_of names a bundle of the block's own source group. cellblock_of names a cell block of the block's own depth band.
All inputs are finite; a program needn't handle non-finite values.
Results may differ from a plain program's by a relative error of at most 0.0059.
Values may be sent and summed in bfloat16 or wider, within the bound.
A program may use at most 64 MiB of HBM per device.

v0:
```python
import jax
import jax.numpy as jnp
from jax import lax
from jax.sharding import PartitionSpec as P

CBLK = 128


def block_products(sensitivity, cellblock_of, probe):
    columns = probe.reshape(-1, CBLK, probe.shape[1])[cellblock_of]
    return jnp.einsum("krc,kce->kre", sensitivity, columns, preferred_element_type=jnp.float32)


def adjoint_part(sensitivity, bundle_of, cellblock_of, resid_all, cell_blocks):
    rows = resid_all[bundle_of]
    contrib = jnp.einsum("krc,kre->kce", sensitivity, rows, preferred_element_type=jnp.float32)
    summed = jax.ops.segment_sum(contrib, cellblock_of, num_segments=cell_blocks)
    return summed.reshape(cell_blocks * CBLK, rows.shape[2])


def per_device(sensitivity, bundle_of, cellblock_of, state, prior_velocity, observed, pick_weight):
    nband = lax.axis_size("band")
    owned = observed.shape[0]
    bundles = owned * nband
    cell_blocks = state.shape[0] // CBLK

    def residual_pass(probe):
        prod = block_products(sensitivity, cellblock_of, probe)
        partial_value = jax.ops.segment_sum(prod, bundle_of, num_segments=bundles)
        pred = lax.psum_scatter(partial_value, "band", scatter_dimension=0, tiled=True)
        resid = pick_weight[:, :, None] * (pred - observed[:, :, None])
        resid_all = lax.all_gather(resid.astype(jnp.bfloat16), "band", axis=0, tiled=True)
        return (resid, adjoint_part(sensitivity, bundle_of, cellblock_of, resid_all, cell_blocks))

    probe1 = (state + 0.5 * prior_velocity).astype(jnp.bfloat16)
    res1, part1 = residual_pass(probe1)

    def summed_grad(part):
        return lax.psum(part, "shot")

    grad1 = summed_grad(part1)
    middle = state + 0.5 * (prior_velocity - 0.5 * grad1)
    probe2 = (middle + 0.5 * prior_velocity).astype(jnp.bfloat16)
    res2, part2 = residual_pass(probe2)
    grad2 = summed_grad(part2)
    new_state = state + 0.5 * (prior_velocity - 0.25 * (grad1 + grad2))
    return (new_state, res2)


def solution(mesh):
    in_specs = (
        P(("shot", "band"), None, None),
        P(("shot", "band")),
        P(("shot", "band")),
        P("band", None),
        P("band", None),
        P(("shot", "band"), None),
        P(("shot", "band"), None),
    )
    out_specs = (P("band", None), P(("shot", "band"), None, None))
    return jax.shard_map(
        per_device, mesh=mesh, in_specs=in_specs, out_specs=out_specs, check_vma=False
    )
```

profile of v0, /device:TPU:2, one launch (start us, length us, event | category | flops | bytes accessed | tf_op | source)
XLA Modules:
  0.0 845.8 jit_solution(9297075635177994917)
XLA Ops:
  7.2 0.0 copy-start
  7.2 0.0 reduce-scatter.3.cloned.1.call-start
  7.2 0.8 compare_select_fusion.1
  8.0 1.7 add_convert_fusion.1
  9.7 2.2 gather_fusion
  11.8 5.2 convolution_bitcast_fusion.3
  17.0 5.6 copy.28
  22.6 1.6 broadcast.21.clone
  24.2 13.5 %scatter_fusion = f32[32,128,128]{2,1,0:T(8,128)} fusion(f32[32,128,128]{2,1,0:T(8,128)} %broadcast.21.clone, s32[64]{0:T(128)S(1)} %copy-done.3, f32[64,128,128]{2,1,0:T(8,128)} %copy.28), kind=kCustom, calls=%fused_computation.4 | custom fusion | flops 1048576 | bytes 12583168 | tf_op jit(solution)/shard_map/scatter-add | solution.py:29
  37.7 0.0 reduce-scatter.3.cloned.1.call-update
  37.7 0.0 all-gather.3.cloned.1.call-start
  37.8 218.6 %reduce-scatter.3.cloned.1.call-done = f32[1,128,128]{2,1,0:T(8,128)} async-done(((f32[32,128,128]{2,1,0:T(8,128)}), f32[1,128,128]{2,1,0:T(8,128)}) %reduce-scatter.3.cloned.1.call-update) | async-done | bytes 65552 | tf_op jit(solution)/shard_map/reduce_scatter | solution.py:30
  256.4 1.6 multiply_convert_fusion
  257.9 0.0 all-gather.3.cloned.1.call-update
  257.9 0.0 all-reduce.3.cloned.1.call-start
  258.0 76.1 %all-gather.3.cloned.1.call-done = bf16[32,128,128]{2,1,0:T(8,128)(2,1)} async-done(((bf16[1,128,128]{2,1,0:T(8,128)(2,1)}), bf16[32,128,128]{2,1,0:T(8,128)(2,1)}) %all-gather.3.cloned.1.call-update) | async-done | bytes 1048592 | tf_op jit(solution)/shard_map/all_gather | solution.py:32
  334.1 3.4 gather_fusion.1
  337.5 4.4 convolution_bitcast_fusion.2
  341.9 5.6 copy.30
  347.5 0.1 broadcast.20.clone
  347.6 8.8 %scatter_fusion.1 = f32[16,128,128]{2,1,0:T(8,128)S(1)} fusion(f32[16,128,128]{2,1,0:T(8,128)S(1)} %broadcast.20.clone, s32[64]{0:T(128)S(1)} %copy-done.6, f32[64,128,128]{2,1,0:T(8,128)} %copy.30), kind=kCustom, calls=%fused_computation.5 | custom fusion | flops 1048576 | bytes 12583168 | tf_op jit(solution)/shard_map/scatter-add | solution.py:17
  356.4 0.0 copy-start.2
  356.4 1.0 copy-done.2
  357.4 0.0 all-reduce.3.cloned.1.call-update
  357.4 0.0 reduce-scatter.5.cloned.1.call-start
  357.5 66.3 %all-reduce.3.cloned.1.call-done = f32[2048,128]{1,0:T(8,128)} async-done(((f32[2048,128]{1,0:T(8,128)}), f32[2048,128]{1,0:T(8,128)}) %all-reduce.3.cloned.1.call-update) | async-done | bytes 1048592 | tf_op jit(solution)/shard_map/psum | solution.py:39
  423.8 2.1 add_convert_fusion
  425.9 2.2 gather_fusion.2
  428.0 5.2 convolution_bitcast_fusion.1
  433.2 5.6 copy.32
  438.8 1.6 broadcast.21
  440.4 13.5 %scatter_fusion.2 = f32[32,128,128]{2,1,0:T(8,128)} fusion(f32[32,128,128]{2,1,0:T(8,128)} %broadcast.21, s32[64]{0:T(128)S(1)} %copy-done.3, f32[64,128,128]{2,1,0:T(8,128)} %copy.32), kind=kCustom, calls=%fused_computation.6 | custom fusion | flops 1048576 | bytes 12583168 | tf_op jit(solution)/shard_map/scatter-add | solution.py:29
  453.9 0.0 reduce-scatter.5.cloned.1.call-update
  453.9 0.0 all-gather.5.cloned.1.call-start
  454.0 214.7 %reduce-scatter.5.cloned.1.call-done = f32[1,128,128]{2,1,0:T(8,128)} async-done(((f32[32,128,128]{2,1,0:T(8,128)}), f32[1,128,128]{2,1,0:T(8,128)}) %reduce-scatter.5.cloned.1.call-update) | async-done | bytes 65552 | tf_op jit(solution)/shard_map/reduce_scatter | solution.py:30
  668.7 1.6 fusion
  670.2 0.0 all-gather.5.cloned.1.call-update
  670.3 0.2 all-reduce.5.cloned.1.call-start
  670.5 75.5 %all-gather.5.cloned.1.call-done = bf16[32,128,128]{2,1,0:T(8,128)(2,1)} async-done(((bf16[1,128,128]{2,1,0:T(8,128)(2,1)}), bf16[32,128,128]{2,1,0:T(8,128)(2,1)}) %all-gather.5.cloned.1.call-update) | async-done | bytes 1048592 | tf_op jit(solution)/shard_map/all_gather | solution.py:32
  746.0 3.4 gather_fusion.3
  749.4 4.4 convolution_bitcast_fusion
  753.8 5.6 copy.34
  759.4 0.1 broadcast.20
  759.5 8.8 %scatter_fusion.3 = f32[16,128,128]{2,1,0:T(8,128)S(1)} fusion(f32[16,128,128]{2,1,0:T(8,128)S(1)} %broadcast.20, s32[64]{0:T(128)S(1)} %copy-done.6, f32[64,128,128]{2,1,0:T(8,128)} %copy.34), kind=kCustom, calls=%fused_computation.7 | custom fusion | flops 1048576 | bytes 12583168 | tf_op jit(solution)/shard_map/scatter-add | solution.py:17
  768.3 1.0 copy-done.1
  769.2 0.0 all-reduce.5.cloned.1.call-update
  769.3 66.3 %all-reduce.5.cloned.1.call-done = f32[2048,128]{1,0:T(8,128)} async-done(((f32[2048,128]{1,0:T(8,128)}), f32[2048,128]{1,0:T(8,128)}) %all-reduce.5.cloned.1.call-update) | async-done | bytes 1048592 | tf_op jit(solution)/shard_map/psum | solution.py:39
  835.6 3.3 multiply_add_fusion
  (13 shorter events, 0.0 us)
Async XLA Ops:
  7.2 4.7 copy-start
  7.2 249.2 %reduce-scatter.3.cloned.1.call-start = ((), (), s32[]{:S(2)}) async-start(), calls=%async_computation.2 | async-start | bytes 2162688 | tf_op jit(solution)/shard_map/reduce_scatter | solution.py:30
  22.6 1.6 copy-start.3
  37.7 218.6 %copy-start.4 = (f32[1,128]{1,0:T(1,128)S(1)}, f32[1,128]{1,0:T(1,128)}, u32[]{:S(2)}) copy-start(f32[1,128]{1,0:T(1,128)} %param.12) | copy-start | bytes 1540
  37.7 218.6 %copy-start.5 = (f32[1,128]{1,0:T(1,128)S(1)}, f32[1,128]{1,0:T(1,128)}, u32[]{:S(2)}) copy-start(f32[1,128]{1,0:T(1,128)} %param.13) | copy-start | bytes 1540
  37.7 296.4 %all-gather.3.cloned.1.call-start = ((), (), s32[]{:S(2)}) async-start(), calls=%async_computation.3 | async-start | bytes 1081344 | tf_op jit(solution)/shard_map/all_gather | solution.py:32
  257.9 165.8 %all-reduce.3.cloned.1.call-start = ((), (), s32[]{:S(2)}) async-start(), calls=%async_computation.4 | async-start | bytes 2097152 | tf_op jit(solution)/shard_map/psum | solution.py:39
  341.9 5.7 copy-start.6
  356.4 1.0 copy-start.2
  357.4 311.3 %reduce-scatter.5.cloned.1.call-start = ((), (), s32[]{:S(2)}) async-start(), calls=%async_computation.5 | async-start | bytes 2162688 | tf_op jit(solution)/shard_map/reduce_scatter | solution.py:30
  453.9 292.1 %all-gather.5.cloned.1.call-start = ((), (), s32[]{:S(2)}) async-start(), calls=%async_computation.6 | async-start | bytes 1081344 | tf_op jit(solution)/shard_map/all_gather | solution.py:32
  670.3 165.3 %all-reduce.5.cloned.1.call-start = ((), (), s32[]{:S(2)}) async-start(), calls=%async_computation.7 | async-start | bytes 2097152 | tf_op jit(solution)/shard_map/psum | solution.py:39
  768.3 1.0 copy-start.1
Sparse Core Ops, SparseCore 0:
  37.9 218.4 reduce-scatter.2
  259.9 74.2 all-gather.2
  357.5 66.1 all-reduce.2
  454.0 214.5 reduce-scatter.4
  671.7 74.3 all-gather.4
  769.4 66.1 all-reduce.4
where the time goes:
time: 847 us; the launch traced here: 846 us
  waiting for transfers between devices  718 us (85%)
  other arithmetic  55.7 us (7%)
  local copies, waits for them, and re-layouts  38.7 us (5%)
  matrix products  19.1 us (2%)
  between operations  14.2 us (2%)
    reduce_scatter x2, waiting for transfers between devices, residual_pass(): lax.psum_scatter(partial_value, 'band', scatter_dimension=0, tiled=True)  433 us
    all_gather x2, waiting for transfers between devices, residual_pass(): lax.all_gather(resid.astype(jnp.bfloat16), 'band', axis=0, tiled=True)  152 us
    psum x2, waiting for transfers between devices, summed_grad(): return lax.psum(part, 'shot')  133 us
    scatter-add x2, other arithmetic, residual_pass(): partial_value = jax.ops.segment_sum(prod, bundle_of, num_segments=bundles)  27 us
    scatter-add x2, other arithmetic, adjoint_part(): jax.ops.segment_sum(contrib, cellblock_of, num_segments=cell_blocks)  17.6 us
  transfers between devices with their start and end apart: 6, of which 6 were waited for; matrix products, arithmetic and copies ran while one was open for 0% of the time, Pallas kernels for 0%

commit v1 on v0

--- a/solution.py
+++ b/solution.py
@@ -29,7 +29,15 @@
         partial_value = jax.ops.segment_sum(prod, bundle_of, num_segments=bundles)
         pred = lax.psum_scatter(partial_value, "band", scatter_dimension=0, tiled=True)
         resid = pick_weight[:, :, None] * (pred - observed[:, :, None])
-        resid_all = lax.all_gather(resid.astype(jnp.bfloat16), "band", axis=0, tiled=True)
+        resid_all = jnp.concatenate(
+            lax.all_to_all(
+                jnp.stack([resid.astype(jnp.bfloat16)] * lax.axis_size("band")),
+                axis_name="band",
+                split_axis=0,
+                concat_axis=0,
+            ),
+            0,
+        )
         return (resid, adjoint_part(sensitivity, bundle_of, cellblock_of, resid_all, cell_blocks))
 
     probe1 = (state + 0.5 * prior_velocity).astype(jnp.bfloat16)

time: 847 us -> 751 us (0.89)
  waiting for transfers between devices: 718 us -> 586 us
  blocking collectives: 0 us -> 28.7 us
    all_gather x2 -> x0, waiting for transfers between devices: 152 us -> none  [residual_pass(): lax.all_gather(resid.astype(jnp.bfloat16), 'band', axis=0, tiled=True)]
    all_to_all x0 -> x1, blocking collectives: none -> 28.7 us  [residual_pass(): lax.all_to_all(jnp.stack([resid.astype(jnp.bfloat16)] * lax.axis_size('ba...]
    all_to_all x0 -> x1, waiting for transfers between devices: none -> 20.8 us  [residual_pass(): lax.all_to_all(jnp.stack([resid.astype(jnp.bfloat16)] * lax.axis_size('ba...]
  transfers between devices with their start and end apart: 6 -> 5, of which waited for: 6 -> 5; matrix products, arithmetic and copies ran while one was open for 0% -> 0% of each run, Pallas kernels for 0% -> 0%
where the time goes in v1:
time: 751 us; the launch traced here: 749 us
  waiting for transfers between devices  586 us (78%)
  other arithmetic  55.1 us (7%)
  local copies, waits for them, and re-layouts  37.7 us (5%)
  blocking collectives  28.7 us (4%)
  matrix products  19.1 us (3%)
  between operations  13.9 us (2%)
  starting transfers between devices  8.2 us (1%)
    reduce_scatter x2, waiting for transfers between devices, residual_pass(): lax.psum_scatter(partial_value, 'band', scatter_dimension=0, tiled=True)  433 us
    psum x2, waiting for transfers between devices, summed_grad(): return lax.psum(part, 'shot')  133 us
    all_to_all x1, blocking collectives, residual_pass(): lax.all_to_all(jnp.stack([resid.astype(jnp.bfloat16)] * lax.axis_size('ba...  28.7 us
    scatter-add x2, other arithmetic, residual_pass(): partial_value = jax.ops.segment_sum(prod, bundle_of, num_segments=bundles)  27.1 us
    all_to_all x1, waiting for transfers between devices, residual_pass(): lax.all_to_all(jnp.stack([resid.astype(jnp.bfloat16)] * lax.axis_size('ba...  20.8 us
    scatter-add x2, other arithmetic, adjoint_part(): jax.ops.segment_sum(contrib, cellblock_of, num_segments=cell_blocks)  17.6 us
  transfers between devices with their start and end apart: 5, of which 5 were waited for; matrix products, arithmetic and copies ran while one was open for 0% of the time, Pallas kernels for 0%

profile of v1, /device:TPU:2, one launch (start us, length us, event | category | flops | bytes accessed | tf_op | source)
XLA Modules:
  0.0 749.1 jit_solution(2963647071339239053)
XLA Ops:
  7.2 0.0 copy-start
  7.2 0.0 reduce-scatter.3.cloned.1.call-start
  7.2 0.8 compare_select_fusion.1
  8.0 1.7 add_convert_fusion.1
  9.7 2.2 gather_fusion
  11.9 5.2 convolution_bitcast_fusion.3
  17.0 5.6 copy.22
  22.6 1.6 broadcast.27.clone
  24.2 13.5 %scatter_fusion = f32[32,128,128]{2,1,0:T(8,128)} fusion(f32[32,128,128]{2,1,0:T(8,128)} %broadcast.27.clone, s32[64]{0:T(128)S(1)} %copy-done.3, f32[64,128,128]{2,1,0:T(8,128)} %copy.22), kind=kCustom, calls=%fused_computation.4 | custom fusion | flops 1048576 | bytes 12583168 | tf_op jit(solution)/shard_map/scatter-add | solution.py:29
  37.8 0.0 reduce-scatter.3.cloned.1.call-update
  37.8 218.0 %reduce-scatter.3.cloned.1.call-done = f32[1,128,128]{2,1,0:T(8,128)} async-done(((f32[32,128,128]{2,1,0:T(8,128)}), f32[1,128,128]{2,1,0:T(8,128)}) %reduce-scatter.3.cloned.1.call-update) | async-done | bytes 65552 | tf_op jit(solution)/shard_map/reduce_scatter | solution.py:30
  255.8 0.9 fusion
  256.7 1.2 stack.4
  257.9 8.0 %all-to-all-start = ((bf16[32,1,128,128]{3,2,1,0:T(8,128)(2,1)}), bf16[32,1,128,128]{3,2,1,0:T(8,128)(2,1)S(1)}, u32[]{:S(2)}, u32[]{:S(2)}) async-start(bf16[32,1,128,128]{3,2,1,0:T(8,128)(2,1)} %stack.4), calls=%async_computation.1 | async-start | bytes 2097152 | tf_op jit(solution)/shard_map/all_to_all | solution.py:33
  266.0 0.0 all-reduce.3.cloned.1.call-start
  266.1 20.8 %all-to-all-done = bf16[32,1,128,128]{3,2,1,0:T(8,128)(2,1)S(1)} async-done(((bf16[32,1,128,128]{3,2,1,0:T(8,128)(2,1)}), bf16[32,1,128,128]{3,2,1,0:T(8,128)(2,1)S(1)}, u32[]{:S(2)}, u32[]{:S(2)}) %all-to-all-start) | async-done | bytes 1048608 | tf_op jit(solution)/shard_map/all_to_all | solution.py:33
  286.9 2.1 gather_fusion.1
  289.0 4.4 convolution_bitcast_fusion.2
  293.4 5.6 copy.24
  299.0 0.1 broadcast.26.clone
  299.1 8.8 %scatter_fusion.1 = f32[16,128,128]{2,1,0:T(8,128)S(1)} fusion(f32[16,128,128]{2,1,0:T(8,128)S(1)} %broadcast.26.clone, s32[64]{0:T(128)S(1)} %copy-done.6, f32[64,128,128]{2,1,0:T(8,128)} %copy.24), kind=kCustom, calls=%fused_computation.5 | custom fusion | flops 1048576 | bytes 12583168 | tf_op jit(solution)/shard_map/scatter-add | solution.py:17
  307.9 0.0 copy-start.2
  308.0 1.0 copy-done.2
  308.9 0.0 all-reduce.3.cloned.1.call-update
  308.9 0.0 reduce-scatter.5.cloned.1.call-start
  309.0 66.4 %all-reduce.3.cloned.1.call-done = f32[2048,128]{1,0:T(8,128)} async-done(((f32[2048,128]{1,0:T(8,128)}), f32[2048,128]{1,0:T(8,128)}) %all-reduce.3.cloned.1.call-update) | async-done | bytes 1048592 | tf_op jit(solution)/shard_map/psum | solution.py:47
  375.4 2.1 add_convert_fusion
  377.5 2.2 gather_fusion.2
  379.7 5.2 convolution_bitcast_fusion.1
  384.9 5.6 copy.26
  390.5 1.6 broadcast.27
  392.1 13.5 %scatter_fusion.2 = f32[32,128,128]{2,1,0:T(8,128)} fusion(f32[32,128,128]{2,1,0:T(8,128)} %broadcast.27, s32[64]{0:T(128)S(1)} %copy-done.3, f32[64,128,128]{2,1,0:T(8,128)} %copy.26), kind=kCustom, calls=%fused_computation.6 | custom fusion | flops 1048576 | bytes 12583168 | tf_op jit(solution)/shard_map/scatter-add | solution.py:29
  405.6 0.0 reduce-scatter.5.cloned.1.call-update
  405.6 0.0 all-reduce.5.cloned.1.call-start
  405.7 214.6 %reduce-scatter.5.cloned.1.call-done = f32[1,128,128]{2,1,0:T(8,128)} async-done(((f32[32,128,128]{2,1,0:T(8,128)}), f32[1,128,128]{2,1,0:T(8,128)}) %reduce-scatter.5.cloned.1.call-update) | async-done | bytes 65552 | tf_op jit(solution)/shard_map/reduce_scatter | solution.py:30
  620.3 1.6 convert_bitcast_fusion
  621.8 0.2 stack.5
  622.1 28.7 %all_to_all.10 = bf16[32,1,128,128]{3,2,1,0:T(8,128)(2,1)S(1)} all-to-all(bf16[32,1,128,128]{3,2,1,0:T(8,128)(2,1)S(1)} %stack.5), channel_id=1, replica_groups=mesh['shot'=8,'band'=32] {'band'}, dimensions={0} | all-to-all | bytes 2097152 | tf_op jit(solution)/shard_map/all_to_all | solution.py:33
  650.8 2.1 gather_fusion.3
  652.9 4.4 convolution_bitcast_fusion
  657.3 5.6 copy.28
  662.9 0.1 broadcast.26
  663.0 8.8 %scatter_fusion.3 = f32[16,128,128]{2,1,0:T(8,128)S(1)} fusion(f32[16,128,128]{2,1,0:T(8,128)S(1)} %broadcast.26, s32[64]{0:T(128)S(1)} %copy-done.6, f32[64,128,128]{2,1,0:T(8,128)} %copy.28), kind=kCustom, calls=%fused_computation.7 | custom fusion | flops 1048576 | bytes 12583168 | tf_op jit(solution)/shard_map/scatter-add | solution.py:17
  671.8 0.0 copy-start.1
  671.8 1.0 copy-done.1
  672.8 0.0 all-reduce.5.cloned.1.call-update
  672.8 66.5 %all-reduce.5.cloned.1.call-done = f32[2048,128]{1,0:T(8,128)} async-done(((f32[2048,128]{1,0:T(8,128)}), f32[2048,128]{1,0:T(8,128)}) %all-reduce.5.cloned.1.call-update) | async-done | bytes 1048592 | tf_op jit(solution)/shard_map/psum | solution.py:47
  739.3 3.3 multiply_add_fusion
  (12 shorter events, 0.0 us)
Async XLA Ops:
  7.2 4.7 copy-start
  7.2 248.6 %reduce-scatter.3.cloned.1.call-start = ((), (), s32[]{:S(2)}) async-start(), calls=%async_computation.4 | async-start | bytes 2162688 | tf_op jit(solution)/shard_map/reduce_scatter | solution.py:30
  22.6 1.6 copy-start.3
  37.7 218.0 %copy-start.4 = (f32[1,128]{1,0:T(1,128)S(1)}, f32[1,128]{1,0:T(1,128)}, u32[]{:S(2)}) copy-start(f32[1,128]{1,0:T(1,128)} %param.12) | copy-start | bytes 1540
  37.8 218.0 %copy-start.5 = (f32[1,128]{1,0:T(1,128)S(1)}, f32[1,128]{1,0:T(1,128)}, u32[]{:S(2)}) copy-start(f32[1,128]{1,0:T(1,128)} %param.13) | copy-start | bytes 1540
  257.9 29.0 %all-to-all-start = ((bf16[32,1,128,128]{3,2,1,0:T(8,128)(2,1)}), bf16[32,1,128,128]{3,2,1,0:T(8,128)(2,1)S(1)}, u32[]{:S(2)}, u32[]{:S(2)}) async-start(bf16[32,1,128,128]{3,2,1,0:T(8,128)(2,1)} %stack.4), calls=%async_computation.1 | async-start | bytes 2097152 | tf_op jit(solution)/shard_map/all_to_all | solution.py:33
  266.0 109.5 %all-reduce.3.cloned.1.call-start = ((), (), s32[]{:S(2)}) async-start(), calls=%async_computation.5 | async-start | bytes 2097152 | tf_op jit(solution)/shard_map/psum | solution.py:47
  293.4 5.7 copy-start.6
  307.9 1.0 copy-start.2
  308.9 311.3 %reduce-scatter.5.cloned.1.call-start = ((), (), s32[]{:S(2)}) async-start(), calls=%async_computation.6 | async-start | bytes 2162688 | tf_op jit(solution)/shard_map/reduce_scatter | solution.py:30
  405.6 333.6 %all-reduce.5.cloned.1.call-start = ((), (), s32[]{:S(2)}) async-start(), calls=%async_computation.7 | async-start | bytes 2097152 | tf_op jit(solution)/shard_map/psum | solution.py:47
  671.8 1.0 copy-start.1
Sparse Core Ops, SparseCore 0:
  37.9 217.8 reduce-scatter.2
  309.1 66.3 all-reduce.2
  405.7 214.4 reduce-scatter.4
  672.9 66.2 all-reduce.4
